TPU v7x, 32 devices: a whole 2x2x4 slice. The times are simulated.
32 devices in a mesh: seq: 8 (over y, x, core), dp: 4 (over z).
Axes of the slice: x: 2, y: 2, z: 4, core: 2. Of those that a mesh axis runs over, the one named last changes fastest.
Arguments:
- queries: bfloat16 [4, 1024, 2048], P('dp', 'seq'), may hold values from -6 to 6
- keys_in: bfloat16 [4, 1024, 2048], P('dp', 'seq'), may hold values from -9 to 9
- values_in: bfloat16 [4, 1024, 2048], P('dp', 'seq'), may hold values from -6 to 6
- inputs: bfloat16 [4, 1024, 2048], P('dp', 'seq'), may hold values from -6 to 6
- target: bfloat16 [4, 1024, 2048], P('dp', 'seq'), may hold values from -4 to 4
- gate_weight: bfloat16 [2048, 16], replicated, may hold values from -0.125 to 0.125
- beta_bias: float32 [16], replicated, may hold values from -9 to 1.5
Outputs:
- output: bfloat16 [4, 1024, 2048], P('dp', 'seq')
- grad_queries: bfloat16 [4, 1024, 2048], P('dp', 'seq')
- grad_keys: bfloat16 [4, 1024, 2048], P('dp', 'seq')
- grad_values: bfloat16 [4, 1024, 2048], P('dp', 'seq')
- grad_weight: float32 [2048, 16], replicated
All inputs are finite; a program needn't handle non-finite values.
Results may differ from a plain program's by a relative error of at most 0.0035.
Values sent between devices are 32-bit elements; how exact they have to be, the bound alone decides.
No kernel may reach another device: no remote copies, remote signals or barrier semaphores. Data moves between devices by JAX's collectives and lax.ppermute only.
A program may use at most 256 MiB of HBM per device.

v0:
```python
import math

import jax
import jax.numpy as jnp
from jax import lax
from jax.sharding import PartitionSpec as P

BLOCK = 128


epsilon = 1e-06
highest_precision = lax.Precision.HIGHEST


def carried_in(value, axis, join, neutral, backward):
    count, mine = (lax.axis_size(axis), lax.axis_index(axis))
    pieces = jax.tree.map(lambda part: lax.all_gather(part, axis), value)
    if backward:
        pieces = jax.tree.map(lambda part: part[::-1], pieces)
        mine = count - 1 - mine
    total = jax.tree.map(
        lambda part, zero: jnp.full_like(part, 0) + jnp.asarray(zero, part.dtype), value, neutral
    )

    def lap(position, total):
        longer = join(total, jax.tree.map(lambda part: part[position], pieces))
        return jax.tree.map(lambda new, old: jnp.where(position < mine, new, old), longer, total)

    return lax.fori_loop(0, count - 1, lap, total)


def unit_rows(matrix):
    return matrix * lax.rsqrt(jnp.sum(matrix * matrix, axis=-1, keepdims=True) + epsilon)


def block_terms(queries, keys_in, values_in, logits):
    length = queries.shape[0]
    head_count = logits.shape[1]
    head_width = queries.shape[1] // head_count
    blocks = length // BLOCK

    def arrange(matrix):
        return matrix.reshape(blocks, BLOCK, head_count, head_width).transpose(0, 2, 1, 3)

    query_unit = unit_rows(arrange(queries.astype(jnp.float32)))
    key_unit = unit_rows(arrange(keys_in.astype(jnp.float32)))
    value_rows = arrange(values_in.astype(jnp.float32))
    strength = (
        (0.5 * jax.nn.sigmoid(logits))
        .reshape(blocks, BLOCK, head_count)
        .transpose(0, 2, 1)[..., None]
    )
    key_gram = jnp.einsum("nhik,nhjk->nhij", key_unit, key_unit, precision=highest_precision)
    lower_mask = jnp.tril(jnp.ones((BLOCK, BLOCK), jnp.float32), -1)
    system = jnp.eye(BLOCK, dtype=jnp.float32) + lower_mask * strength * key_gram
    right_side = jnp.concatenate([strength * key_unit, strength * value_rows], axis=-1)
    solved = jax.scipy.linalg.solve_triangular(system, right_side, lower=True)
    write_keys = solved[..., :head_width]
    write_values = solved[..., head_width:]
    inclusive = jnp.tril(jnp.ones((BLOCK, BLOCK), jnp.float32))
    scores = inclusive * jnp.einsum(
        "nhik,nhjk->nhij", query_unit, key_unit, precision=highest_precision
    )
    return (query_unit, key_unit, write_keys, write_values, scores)


def state_pass(terms, entry_state):

    def state_advance(carried_state, block_parts):
        block_queries, block_keys, write_keys, write_values, score_block = block_parts
        delta_correction = write_values - jnp.einsum(
            "fbi,fir->fbr", write_keys, carried_state, precision=highest_precision
        )
        produced_output = jnp.einsum(
            "fbi,fir->fbr", block_queries, carried_state, precision=highest_precision
        )
        produced_output = produced_output + jnp.einsum(
            "hcj,hjv->hcv", score_block, delta_correction, precision=highest_precision
        )
        carried_state = carried_state + jnp.einsum(
            "nrm,nrp->nmp", block_keys, delta_correction, precision=highest_precision
        )
        return (carried_state, produced_output)

    final_state, produced_output = lax.scan(state_advance, entry_state, terms)
    blocks, head_count, rows_block, head_width = produced_output.shape
    flat = produced_output.transpose(0, 2, 1, 3).reshape(
        blocks * rows_block, head_count * head_width
    )
    return (flat, final_state)


def transition_maps(terms, identity):
    query_unit, key_unit, write_keys, write_values, scores = terms
    head_width = identity.shape[-1]
    joined = jnp.concatenate([identity, jnp.zeros_like(identity)], axis=-1)

    def transition_advance(carried_state, block_parts):
        block_keys, key_portion, value_part = block_parts
        written_update = jnp.concatenate([jnp.zeros_like(value_part), value_part], axis=-1)
        delta_correction = written_update - jnp.einsum(
            "fbi,fir->fbr", key_portion, carried_state, precision=highest_precision
        )
        carried_state = carried_state + jnp.einsum(
            "nrm,nrp->nmp", block_keys, delta_correction, precision=highest_precision
        )
        return (carried_state, None)

    joined = lax.scan(transition_advance, joined, (key_unit, write_keys, write_values))[0]
    return (joined[..., :head_width], joined[..., head_width:])


def apply_map(matrix, offset, carried_state):
    return jnp.einsum("hij,hjk->hik", matrix, carried_state, precision=highest_precision) + offset


def compose(earlier, later):
    matrix = jnp.einsum("hij,hjk->hik", later[0], earlier[0], precision=highest_precision)
    return (matrix, apply_map(later[0], later[1], earlier[1]))


def shards(queries, keys_in, values_in, inputs, target, gate_weight, beta_bias):
    query_rows = queries[0]
    key_rows = keys_in[0]
    value_rows = values_in[0]
    input_rows = inputs[0]
    target_rows = target[0]
    head_count = gate_weight.shape[1]
    head_width = query_rows.shape[1] // head_count
    logits = jnp.dot(input_rows, gate_weight, preferred_element_type=jnp.float32) + beta_bias
    terms, pull_terms = jax.vjp(block_terms, query_rows, key_rows, value_rows, logits)
    identity = jnp.broadcast_to(
        jnp.eye(head_width, dtype=jnp.float32), (head_count, head_width, head_width)
    )
    zero_state = jnp.zeros((head_count, head_width, head_width), jnp.float32)
    transition, offset = transition_maps(terms, identity)
    entry_state = carried_in((transition, offset), "seq", compose, (identity, zero_state), False)[1]
    (produced_output, final_state), pull_state = jax.vjp(state_pass, terms, entry_state)
    rounded = lax.optimization_barrier(produced_output.astype(jnp.bfloat16))
    cotangent = rounded.astype(jnp.float32) - target_rows.astype(jnp.float32)
    pull_entry = jax.vjp(lambda carried_state: state_pass(terms, carried_state)[0], entry_state)[1]
    entry_grad = pull_entry(cotangent)[0]
    adjoint = jnp.swapaxes(transition, 1, 2)
    leaving = carried_in((adjoint, entry_grad), "seq", compose, (identity, zero_state), True)[1]
    grad_terms = pull_state((cotangent, leaving))[0]
    grad_q, grad_k, grad_v, grad_logits = pull_terms(grad_terms)
    local_weight = jnp.dot(
        input_rows.T, grad_logits, preferred_element_type=jnp.float32, precision=highest_precision
    )
    weight_total = lax.psum(local_weight, ("seq", "dp"))
    token_count = input_rows.shape[0] * lax.axis_size("seq") * lax.axis_size("dp")
    scaled = weight_total * (1.0 / math.sqrt(token_count))
    return (rounded[None], grad_q[None], grad_k[None], grad_v[None], scaled)


def solution(mesh):
    placed = (
        P("dp", "seq", None),
        P("dp", "seq", None),
        P("dp", "seq", None),
        P("dp", "seq", None),
        P("dp", "seq", None),
        P(),
        P(),
    )
    return jax.shard_map(
        shards,
        mesh=mesh,
        in_specs=placed,
        out_specs=(
            P("dp", "seq", None),
            P("dp", "seq", None),
            P("dp", "seq", None),
            P("dp", "seq", None),
            P(),
        ),
        check_vma=False,
    )
```

profile of v0, /device:TPU:0, one launch (start us, length us, event | category | flops | bytes accessed | tf_op | source)
XLA Modules:
  0.0 609.5 jit_solution(8568618086074928698)
XLA Ops:
  7.3 1.4 copy.71
  9.6 2.5 fusion.69
  13.2 1.4 fusion.46
  14.5 159.1 %custom-call.10 = f32[16,1,128,128]{2,3,1,0:T(8,128)} custom-call(f32[16,1,128,128]{3,2,1,0:T(8,128)} %fusion.46), custom_call_target="InvertDiagBlocksLowerTriangular" | custom-call | tf_op jit(solution)/shard_map/jvp(jit(_solve_triangular))/vmap()/triangular_solve | solution.py:57
  173.7 1.3 copy.74
  176.8 2.0 fusion.18
  179.0 1.2 copy-done.7
  180.2 1.2 fusion.16
  181.4 2.2 pad_add_fusion
  183.7 1.7 slice_bitcast_fusion.5
  186.2 1.3 copy.86
  187.7 4.5 convolution_multiply_fusion.1
  192.2 50.5 %all-gather.9.cloned.1.call-done = f32[128,128,128]{2,1,0:T(8,128)} async-done(((f32[16,128,128]{2,1,0:T(8,128)}), f32[128,128,128]{2,1,0:T(8,128)}) %all-gather.9.cloned.1.call-update) | async-done | bytes 8388624 | tf_op jit(solution)/shard_map/all_gather | solution.py:17
  242.7 56.3 %all-gather.11.cloned.1.call-done = f32[128,128,128]{2,1,0:T(8,128)} async-done(((f32[16,128,128]{2,1,0:T(8,128)}), f32[128,128,128]{2,1,0:T(8,128)}) %all-gather.11.cloned.1.call-update) | async-done | bytes 8388624 | tf_op jit(solution)/shard_map/all_gather | solution.py:17
  299.0 21.0 %while.18 = (s32[]{:T(128)}, f32[16,128,128]{2,1,0:T(8,128)S(1)}, s32[]{:T(128)}, f32[8,16,128,128]{3,2,1,0:T(8,128)}, f32[8,16,128,128]{3,2,1,0:T(8,128)}, /*index=5*/s32[]{:T(128)}, s32[]{:T(128)}) while((s32[]{:T(128)}, f32[16,128,128]{2,1,0:T(8,128)S(1)}, s32[]{:T(128)}, f32[8,16,128,128]{3,2,1,0:T(8,128)}, ...), condition=%wide.region_3.4_spmd.clone, body=%wide.region_2.3_spmd.clone.sunk | while | flops 403701760 | bytes 7342687 | solution.py:29
  299.1 2.8 fusion.144
  302.0 2.8 fusion.144
  305.0 2.8 fusion.144
  307.9 3.1 fusion.144
  311.1 2.8 fusion.144
  314.0 2.8 fusion.144
  317.0 2.8 fusion.144
  320.0 2.9 convolution_subtract_fusion
  322.9 1.8 fusion.76
  324.7 1.9 fusion.39
  327.7 1.5 fusion.49
  329.6 2.1 fusion.51
  331.7 1.4 fusion.53
  333.2 1.2 fusion.34
  334.8 3.1 convolution_add_fusion.4
  338.0 17.3 %all-gather.13.cloned.1.call-done = f32[128,128,128]{2,1,0:T(8,128)} async-done(((f32[16,128,128]{2,1,0:T(8,128)}), f32[128,128,128]{2,1,0:T(8,128)}) %all-gather.13.cloned.1.call-update) | async-done | bytes 8388624 | tf_op jit(solution)/shard_map/all_gather | solution.py:17
  355.3 7.7 %rev.6 = f32[8,16,128,128]{3,2,1,0:T(8,128)} reverse(f32[8,16,128,128]{3,2,1,0:T(8,128)} %bitcast.250), dimensions={0} | reverse | bytes 16777216 | tf_op jit(solution)/shard_map/rev | solution.py:19
  363.0 4.0 fusion.56
  367.1 2.5 convolution_multiply_fusion
  369.6 2.2 fusion.50
  373.0 38.5 %all-gather.15.cloned.1.call-done = f32[128,128,128]{2,1,0:T(8,128)} async-done(((f32[16,128,128]{2,1,0:T(8,128)}), f32[128,128,128]{2,1,0:T(8,128)}) %all-gather.15.cloned.1.call-update) | async-done | bytes 8388624 | tf_op jit(solution)/shard_map/all_gather | solution.py:17
  411.5 7.8 %rev.7 = f32[8,16,128,128]{3,2,1,0:T(8,128)} reverse(f32[8,16,128,128]{3,2,1,0:T(8,128)} %bitcast.251), dimensions={0} | reverse | bytes 16777216 | tf_op jit(solution)/shard_map/rev | solution.py:19
  419.2 35.5 %while.19 = (s32[]{:T(128)}, f32[16,128,128]{2,1,0:T(8,128)}, s32[]{:T(128)}, f32[8,16,128,128]{3,2,1,0:T(8,128)}, f32[8,16,128,128]{3,2,1,0:T(8,128)}, /*index=5*/s32[]{:T(128)}, s32[]{:T(128)}) while((s32[]{:T(128)}, f32[16,128,128]{2,1,0:T(8,128)}, s32[]{:T(128)}, f32[8,16,128,128]{3,2,1,0:T(8,128)}, ...), condition=%wide.region_6.7_spmd.clone, body=%wide.region_5.6_spmd.clone.sunk | while | flops 403701760 | bytes 7342687 | solution.py:29
  419.3 1.2 copy.156
  420.5 3.8 fusion.147
  424.3 1.2 copy.156
  425.5 3.8 fusion.147
  429.3 1.2 copy.156
  430.5 3.8 fusion.147
  434.3 1.2 copy.156
  435.5 3.8 fusion.147
  439.3 1.2 copy.156
  440.6 3.8 fusion.147
  444.4 1.2 copy.156
  445.6 3.8 fusion.147
  449.4 1.2 copy.156
  450.6 3.8 fusion.147
  454.8 3.0 convolution_add_fusion.2
  457.8 2.3 fusion.118
  460.1 2.3 convolution_bitcast_fusion.3
  462.5 1.9 fusion.30
  464.4 2.2 fusion.21
  466.7 2.5 multiply_reduce_fusion
  469.1 1.4 convolution_bitcast_fusion.1
  470.7 2.2 fusion.38
  472.9 2.5 fusion.37
  475.4 2.2 multiply_reduce_fusion.1
  482.0 119.3 %all-reduce.6.cloned.1.call-done = f32[2048,16]{0,1:T(8,128)} async-done(((f32[2048,16]{0,1:T(8,128)}), f32[2048,16]{0,1:T(8,128)}) %all-reduce.6.cloned.1.call-update) | async-done | bytes 131088 | tf_op jit(solution)/shard_map/psum | solution.py:150
  601.2 1.6 broadcast_multiply_fusion.1
  (105 shorter events, 12.8 us)
Async XLA Ops:
  7.2 5.0 copy-start
  7.2 2.1 copy-start.27
  7.2 235.5 %all-gather.9.cloned.1.call-start = ((), (), s32[]{:S(2)}) async-start(), calls=%async_computation.1 | async-start | bytes 9437184 | tf_op jit(solution)/shard_map/all_gather | solution.py:17
  9.3 2.9 copy-start.28
  9.3 2.9 copy-start.29
  9.5 5.0 copy-start.1
  12.2 1.0 copy-start.22
  175.2 1.0 copy-start.24
  175.2 1.6 copy-start.19
  178.8 1.4 copy-start.7
  185.4 113.6 %all-gather.11.cloned.1.call-start = ((), (), s32[]{:S(2)}) async-start(), calls=%async_computation.2 | async-start | bytes 9437184 | tf_op jit(solution)/shard_map/all_gather | solution.py:17
  186.2 169.1 %all-gather.13.cloned.1.call-start = ((), (), s32[]{:S(2)}) async-start(), calls=%async_computation.3 | async-start | bytes 9437184 | tf_op jit(solution)/shard_map/all_gather | solution.py:17
  187.6 223.9 %all-gather.15.cloned.1.call-start = ((), (), s32[]{:S(2)}) async-start(), calls=%async_computation.4 | async-start | bytes 9437184 | tf_op jit(solution)/shard_map/all_gather | solution.py:17
  320.0 2.9 copy-start.2
  322.9 3.8 copy-start.12
  322.9 1.9 copy-start.17
  327.7 1.9 copy-start.18
  329.4 2.3 copy-start.10
  329.4 2.3 copy-start.3
  331.7 2.6 copy-start.21
  333.2 1.6 copy-start.8
  337.9 263.3 %all-reduce.6.cloned.1.call-start = ((), (), s32[]{:S(2)}) async-start(), calls=%async_computation | async-start | bytes 262144 | tf_op jit(solution)/shard_map/psum | solution.py:150
  363.0 4.0 copy-start.11
  363.0 4.0 copy-start.13
  367.1 2.5 copy-start.4
  369.5 2.2 copy-start.15
  454.8 3.0 copy-start.6
  454.8 3.0 copy-start.14
  460.1 2.3 copy-start.20
  462.4 1.9 copy-start.9
  464.4 2.3 copy-start.23
  469.1 1.4 copy-start.5
  469.1 1.5 copy-start.16
  472.9 2.5 copy-start.25
  479.4 1.3 copy-start.26
Sparse Core Ops, SparseCore 0:
  185.6 57.0 all-gather.8
  244.6 54.3 all-gather.10
  300.9 54.3 all-gather.12
  357.1 54.3 all-gather.14
  478.7 122.4 all-reduce.5
where the time goes:
time: 613 us; the launch traced here: 610 us
  waiting for transfers between devices  283 us (46%)
  other arithmetic  168 us (27%)
  matrix products  104 us (17%)
  local copies, waits for them, and re-layouts  39.5 us (6%)
  between operations  14.7 us (2%)
    all_gather x4, waiting for transfers between devices, carried_in(): pieces = jax.tree.map(lambda part: lax.all_gather(part, axis), value)  163 us
    another operation x3, other arithmetic, block_terms(): solved = jax.scipy.linalg.solve_triangular(system, right_side, lower=True)  161 us
    psum x1, waiting for transfers between devices, shards(): weight_total = lax.psum(local_weight, ('seq', 'dp'))  119 us
    dot_general x14, matrix products, apply_map(): jnp.einsum('hij,hjk->hik', matrix, carried_state, precision=highest_preci...  46.6 us
    rev x2, local copies, waits for them, and re-layouts, carried_in(): pieces = jax.tree.map(lambda part: part[::-1], pieces)  15.5 us
  transfers between devices with their start and end apart: 5, of which 5 were waited for; matrix products, arithmetic and copies ran while one was open for 11% of the time, Pallas kernels for 0%

commit v1 on v0

v1 whole, which is shorter than its diff:
```python
import functools
import math

import jax
import jax.numpy as jnp
from jax import lax
from jax.experimental import pallas as pl
from jax.experimental.pallas import tpu as pltpu
from jax.sharding import PartitionSpec as P

EPSILON = 1e-06
HELD = True
VMEM_BYTES = 16 * 1024 * 1024

NN = (((1,), (0,)), ((), ()))
NT = (((1,), (1,)), ((), ()))
TN = (((0,), (0,)), ((), ()))

f32 = jnp.float32
bf16 = jnp.bfloat16


def split(x):
    if isinstance(x, tuple):
        return x
    if x.dtype == bf16:
        return (x,)
    head = x.astype(bf16)
    return (head, (x - head.astype(f32)).astype(bf16))


def mm(a, b, form):
    a, b = split(a), split(b)
    contract_a, contract_b = form[0][0][0], form[0][1][0]
    many_a, many_b = len(a), len(b)
    left = jnp.concatenate(a, axis=contract_a) if many_a > 1 else a[0]
    right = jnp.concatenate(b, axis=1 - contract_b) if many_b > 1 else b[0]
    if many_a > 1:
        right = jnp.concatenate([right] * many_a, axis=contract_b)
    out = lax.dot_general(left, right, form, preferred_element_type=f32)
    if many_b > 1:
        width = out.shape[1] // many_b
        out = out[:, :width] + out[:, width:]
    return out


def each(function, *lists):
    return [function(*items) for items in zip(*lists)]


def index_pair(rows, columns):
    return (
        lax.broadcasted_iota(jnp.int32, (rows, columns), 0),
        lax.broadcasted_iota(jnp.int32, (rows, columns), 1),
    )


def inverse_factor(x):
    x = x.astype(f32)
    return lax.rsqrt(jnp.sum(x * x, axis=1, keepdims=True) + EPSILON)


def head_slice(ref, head, width):
    return ref[:, head * width : (head + 1) * width]


def column(matrix, index):
    lane = lax.broadcasted_iota(jnp.int32, matrix.shape, 1)
    return jnp.sum(jnp.where(lane == index, matrix, 0.0), axis=1, keepdims=True)


def as_row(x, eye):
    return jnp.sum(jnp.where(eye, x, 0.0), axis=0, keepdims=True)


def unit_inverse(systems, length):
    row, col = index_pair(length, length)
    eye = row == col
    levels = int(math.log2(length))
    low = each(lambda a: a.astype(bf16), systems)
    solved = None
    for level in range(levels):
        same_outer = (row >> (level + 1)) == (col >> (level + 1))
        same_inner = (row >> level) == (col >> level)
        mask = same_outer & jnp.logical_not(same_inner)
        if level == 0:
            solved = each(lambda a: jnp.where(eye, 1.0, -jnp.where(mask, a, 0.0)), systems)
            continue
        known = each(lambda x: x.astype(bf16), solved)
        part = each(lambda a: jnp.where(mask, a, jnp.zeros_like(a)), low)
        middle = each(lambda a, x: mm(a, x, NN).astype(bf16), part, known)
        solved = each(lambda full, x, z: full - mm(x, z, NN), solved, known, middle)
    known = each(lambda x: x.astype(bf16), solved)
    rest = each(lambda a, x: jnp.where(eye, 1.0, 0.0) - x.astype(f32) - mm(a, x, NN), systems, known)
    return each(lambda x, r: x.astype(f32) + mm(x, r.astype(bf16), NN), known, rest)


def chronological(first, own, other):
    own, other = own.astype(f32), other.astype(f32)
    return jnp.where(first, own, other), jnp.where(first, other, own)


def both(first, own_ref, other_ref, group, width):
    pairs = [
        chronological(first, head_slice(own_ref, h, width), head_slice(other_ref, h, width))
        for h in range(group)
    ]
    return [block for pair in pairs for block in pair]


def both_strengths(step, place, first, own_ref, other_ref, group, heads):
    start = place[0] * heads + step * group
    pairs = [
        chronological(first, column(own_ref[...], start + h), column(other_ref[...], start + h))
        for h in range(group)
    ]
    return [block for pair in pairs for block in pair]


def hand_out(first, blocks, own_ref, other_ref, width):
    for h in range(len(blocks) // 2):
        early, late = blocks[2 * h : 2 * h + 2]
        columns = slice(h * width, (h + 1) * width)
        own_ref[:, columns] = jnp.where(first, early, late).astype(own_ref.dtype)
        other_ref[:, columns] = jnp.where(first, late, early).astype(other_ref.dtype)


def deliver(place, refs, share, head, pieces):
    copies, part_share = len(pieces), refs[0].shape[0]
    chips = len(refs) * part_share // share
    slot = head % share
    first = slot // part_share * chips
    for part, piece in enumerate(pieces):
        distance = lax.bitwise_xor(head * copies // share + part, place[1])
        for index, ref in enumerate(refs[first : first + chips]):

            @pl.when(distance == index)
            def _():
                ref[slot % part_share] = piece


def collect(place, refs, scratch):
    chips, part_share = scratch.shape[0], refs[0].shape[0]
    for index, ref in enumerate(refs):
        stage, distance = divmod(index, chips)
        scratch[lax.bitwise_xor(place[1], distance), stage * part_share : (stage + 1) * part_share] = ref[...]


def collected(scratch, head, copies):
    share = scratch.shape[1]
    owner = head * copies // share
    pieces = [scratch[owner + part, head % share] for part in range(copies)]
    return jnp.concatenate(pieces, axis=0) if copies > 1 else pieces[0]


def divide(place, ref, half):
    own = ref[:, pl.ds(pl.multiple_of(place[0] * half, half), half)]
    other = ref[:, pl.ds(pl.multiple_of((1 - place[0]) * half, half), half)]
    return own.astype(f32), other.astype(f32)


def pack_kernel(place, inputs, weight, bias, k, v, beta_out, send, k_out, v_out):
    half = k_out.shape[1]
    heads = weight.shape[0]
    logits = lax.dot_general(inputs[...], weight[...], NT, preferred_element_type=f32) + bias[...]
    beta = 0.5 / (1.0 + jnp.exp(-logits))
    beta_out[...] = beta
    k_out[...], send[:, :half] = divide(place, k, half)
    v_out[...], send[:, half : 2 * half] = divide(place, v, half)
    send[:, 2 * half :] = jnp.zeros((send.shape[0], send.shape[1] - 2 * half), f32)
    send[:, 2 * half : 2 * half + heads] = beta


def pack_rest_kernel(place, q, target, inputs, after, send, q_out, target_out, inputs_out):
    half = q_out.shape[1]
    q_out[...], send[:, :half] = divide(place, q, half)
    target_out[...], send[:, half : 2 * half] = divide(place, target, half)
    send[:, 2 * half :] = inputs[...].astype(f32)
    inputs_out[...] = inputs[...]


def join_kernel(place, *refs):
    count = len(refs) // 3
    first = place[0] == 0
    for index in range(count):
        own, other, out = refs[2 * index], refs[2 * index + 1], refs[2 * count + index]
        half = own.shape[1]
        early, late = chronological(first, own[...], other[...])
        out[:, :half] = early.astype(bf16)
        out[:, half:] = late.astype(bf16)


def exact(x):
    return x.astype(bf16)


def maps_kernel(
    heads, share, step, place, k, k2, v, v2, beta, beta2, early_out, late_out, early_offset_out, x_out, wk_out, wv_out, *joint_out
):
    first = place[0] == 0
    length = k.shape[0]
    group, width, _ = early_out.shape
    rows = joint_out[0].shape[1] - width
    row, col = index_pair(length, length)
    strict = row > col
    eye = row == col
    kh = both(first, k, k2, group, width)
    b = both_strengths(step, place, first, beta, beta2, group, heads)
    items = list(range(2 * group))
    rk = each(inverse_factor, kh)
    kb = each(exact, kh)
    gram = each(lambda x: mm(x, x, NT), kb)
    system = each(lambda g, b, r: jnp.where(strict, g * (b * r) * as_row(r, eye), 0.0), gram, b, rk)
    x = unit_inverse(system, length)
    wk = each(lambda x, b, r, y: mm(x * as_row(b * r, eye), y, NN), x, b, rk, kb)
    vb = each(exact, both(first, v, v2, group, width))
    wv = each(lambda x, b, y: mm(x * as_row(b, eye), y, NN), x, b, vb)
    for n in items:
        x_out[n // 2, n % 2] = x[n]
        wk_out[n // 2, n % 2] = wk[n]
        wv_out[n // 2, n % 2] = wv[n]
    maps = each(lambda a, r, b: jnp.where(eye, 1.0, 0.0) - mm(a, r * b, TN), kb, rk, wk)
    offsets = each(lambda a, r, y: mm(r * a, y, TN), wv, rk, kb)
    late = [split(maps[2 * h + 1]) for h in range(group)]
    joint = [mm(late[h], maps[2 * h], NN) for h in range(group)]
    offset = [mm(offsets[2 * h], late[h], NT) + offsets[2 * h + 1] for h in range(group)]
    for h in range(group):
        early_out[h] = maps[2 * h]
        late_out[h] = maps[2 * h + 1]
        early_offset_out[h] = offsets[2 * h]
        pieces = [
            jnp.concatenate([joint[h], offset[h][start : start + rows]], axis=0) for start in range(0, width, rows)
        ]
        deliver(place, joint_out, share, step * group + h, pieces)


def queries_kernel(step, place, q, q2, k, k2, wk, wv, early, early_offset, p_out, late_out, qj_out, oj_out):
    first = place[0] == 0
    length = q.shape[0]
    group, width, _ = late_out.shape
    row, col = index_pair(length, length)
    lower = row >= col
    items = list(range(2 * group))
    qh = both(first, q, q2, group, width)
    kh = both(first, k, k2, group, width)
    rq = each(inverse_factor, qh)
    rk = each(lambda x: as_row(inverse_factor(x), row == col), kh)
    qn = each(lambda x, r: x * r, qh, rq)
    p = each(lambda a, r, b, c: jnp.where(lower, r * mm(exact(a), exact(b), NT) * c, 0.0), qh, rq, kh, rk)
    ps = each(split, p)
    qt = [qn[n] - mm(ps[n], wk[n // 2, n % 2], NN) for n in items]
    o = [mm(ps[n], wv[n // 2, n % 2], NN) for n in items]
    for h in range(group):
        late = split(qt[2 * h + 1])
        late_out[h] = qt[2 * h + 1]
        qj_out[h, 0], oj_out[h, 0] = qt[2 * h], o[2 * h]
        qj_out[h, 1] = mm(late, early[h], NN)
        oj_out[h, 1] = o[2 * h + 1] + mm(late, early_offset[h], NT)
    for n in items:
        p_out[n // 2, n % 2] = p[n]


def scan_kernel(reverse, steps, count, place, *refs):
    *arrays, ordered_maps, ordered_offsets, states = refs
    maps, offsets, outs = arrays[:count], arrays[count:-steps], arrays[-steps:]
    share, rows, width = outs[0].shape
    heads = list(range(share))
    collect(place, maps, ordered_maps)
    if offsets:
        collect(place, offsets, ordered_offsets)
    state = [jnp.zeros((rows, width), f32) for _ in heads]
    for index in range(steps):
        n = steps - 1 - index if reverse else index
        for h in heads:
            states[n, h] = state[h]
        offset = [ordered_offsets[n, h] if offsets else ordered_maps[n, h, width:] for h in heads]
        if index == 0:
            state = offset
        elif index < steps - 1:
            form = NN if reverse else NT
            state = [mm(state[h], ordered_maps[n, h, :width], form) + offset[h] for h in heads]
    for distance in range(steps):
        outs[distance][...] = states[lax.bitwise_xor(place[1], distance)]


def output_kernel(heads, share, count, step, place, qj, oj, target, target2, *refs):
    received, refs = refs[:count], refs[count:]
    rounded_out, state_out, *g_out, ordered = refs
    first = place[0] == 0
    group, width, _ = state_out.shape

    collect(place, received, ordered)

    copies = max(1, ordered.shape[0] * ordered.shape[1] // heads)
    state = [collected(ordered, step * group + h, copies) for h in range(group)]
    items = list(range(2 * group))
    goal = both(first, target, target2, group, width)
    ts = each(split, state)
    qs = [split(qj[n // 2, n % 2]) for n in items]
    rounded = [(oj[n // 2, n % 2] + mm(qs[n], ts[n // 2], NT)).astype(bf16) for n in items]
    do = each(lambda a, b: a.astype(f32) - b, rounded, goal)
    dos = each(split, do)

    def stacked(parts, h):
        return tuple(jnp.concatenate(pair, axis=0) for pair in zip(parts[2 * h], parts[2 * h + 1]))

    joint = [mm(stacked(dos, h), stacked(qs, h), TN) for h in range(group)]
    rows = width // copies
    for h in range(group):
        pieces = [joint[h][part * rows : (part + 1) * rows] for part in range(copies)]
        deliver(place, g_out, share, step * group + h, pieces)
        state_out[h] = state[h]
    for n in items:
        rounded_out[n // 2, n % 2] = rounded[n]


def normal_pull(factor, unit, grad):
    return factor * (grad - unit * jnp.sum(unit * grad, axis=1, keepdims=True))


def fresh_kernel(
    step, place, state, early, early_offset, late, wk, wv, p, rounded, target, target2, qt_late, x, k, k2,
    mid_out, f_out, g_late_out, yp_out, xk_out, do_out, out_own, out_other,
):
    first = place[0] == 0
    group, width, _ = state.shape
    items = list(range(2 * group))
    kh = both(first, k, k2, group, width)
    rk = each(inverse_factor, kh)
    kb = each(exact, kh)
    ts = [split(state[h]) for h in range(group)]
    outs = [rounded[n // 2, n % 2].astype(f32) for n in items]
    do = each(lambda a, b: a - b, outs, both(first, target, target2, group, width))
    for n in items:
        do_out[n // 2, n % 2] = do[n]
    do = each(split, do)
    hand_out(first, outs, out_own, out_other, width)
    mid = [mm(ts[h], early[h], NT) + early_offset[h] for h in range(group)]
    g_late = [mm(do[2 * h + 1], qt_late[h], TN) for h in range(group)]
    dfp = [mm(p[n // 2, n % 2], do[n], TN) for n in items]
    ms = each(split, mid)
    f = [wv[n // 2, n % 2] - mm(wk[n // 2, n % 2], ms[n // 2] if n % 2 else ts[n // 2], NT) for n in items]
    for h in range(group):
        mid_out[h] = mid[h]
        g_late_out[h] = g_late[h]
    for n in items:
        f_out[n // 2, n % 2] = f[n]
    kj = [kb[n] if n % 2 else rk[n] * mm(kb[n], late[n // 2], NT) for n in items]
    dfp = [dfp[n] if n % 2 else dfp[n] + rk[n] * mm(kb[n], g_late[n // 2], NT) for n in items]
    xs = [x[n // 2, n % 2] for n in items]
    xk = [mm(rk[n] * xs[n] if n % 2 else xs[n], kj[n], TN) for n in items]
    yp = [mm(xs[n], dfp[n], TN) for n in items]
    for n in items:
        yp_out[n // 2, n % 2] = yp[n]
        xk_out[n // 2, n % 2] = xk[n]


def query_kernel(step, place, state, mid, f, do_all, q, q2, k, k2, gq_own, gq_other, dkp_out):
    first = place[0] == 0
    group, width, _ = state.shape
    length = q.shape[0]
    row, col = index_pair(length, length)
    lower = row >= col
    items = list(range(2 * group))
    qh = both(first, q, q2, group, width)
    rq = each(inverse_factor, qh)
    qn = each(lambda x, r: x * r, qh, rq)
    kh = both(first, k, k2, group, width)
    rk = each(lambda x: as_row(inverse_factor(x), row == col), kh)
    do = [split(do_all[n // 2, n % 2]) for n in items]
    ts = [(mid if n % 2 else state)[n // 2] for n in items]
    dp = [jnp.where(lower, mm(do[n], f[n // 2, n % 2], NT), 0.0) for n in items]
    dq = [mm(do[n], ts[n], NN) + mm(dp[n] * rk[n], exact(kh[n]), NN) for n in items]
    hand_out(first, each(normal_pull, rq, qn, dq), gq_own, gq_other, width)
    for n in items:
        dkp_out[n // 2, n % 2] = mm(rq[n] * dp[n], exact(qh[n]), TN)


def value_kernel(heads, count, step, place, yp, xk, f, beta, beta2, inputs, inputs2, *refs):
    received, refs = refs[:count], refs[count:]
    leaving_out, gw_out, dlogit, ordered = refs
    copies = max(1, ordered.shape[0] * ordered.shape[1] // heads)
    first = place[0] == 0
    group, width, _ = leaving_out.shape

    collect(place, received, ordered)

    leaving = [collected(ordered, step * group + h, copies) for h in range(group)]
    items = list(range(2 * group))
    b = both_strengths(step, place, first, beta, beta2, group, heads)
    hs = each(split, leaving)
    y = [yp[n // 2, n % 2] + mm(xk[n // 2, n % 2], hs[n // 2], NT) for n in items]

    dlogit[...] = jnp.zeros_like(dlogit)

    lane = lax.broadcasted_iota(jnp.int32, dlogit.shape[1:], 1)
    for block in range(2):
        gathered = dlogit[block]
        for h in range(group):
            n = 2 * h + block
            mine = (1.0 - 2.0 * b[n]) * jnp.sum(y[n] * f[h, block], axis=1, keepdims=True)
            gathered = gathered + jnp.where(lane == step * group + h, mine, 0.0)
        dlogit[block] = gathered
    for h in range(group):
        leaving_out[h] = leaving[h]

    own, other = chronological(first, dlogit[0], dlogit[1])
    gw_out[...] = mm(own, inputs[...], TN) + mm(other, inputs2[...].astype(bf16), TN)


def spread_kernel(scale, place, *refs):
    *parts, out = refs
    count, rows = len(parts) // 2, parts[0].shape[0]
    for side, at in ((parts[:count], place[0]), (parts[count:], 1 - place[0])):
        total = add_in_pairs([part[...] for part in side])
        out[pl.ds(pl.multiple_of(at * rows, rows), rows)] = scale * total


def add_in_pairs(parts):
    while len(parts) > 1:
        parts = [a + b for a, b in zip(parts[::2], parts[1::2])]
    return parts[0]


def key_kernel(
    heads, step, place, leaving, late, g_late, state, mid, yp, xk, f, dkp, beta, beta2, k, k2,
    gv_own, gv_other, gk_own, gk_other,
):
    first = place[0] == 0
    group, width, _ = leaving.shape
    length = k.shape[0]
    row, col = index_pair(length, length)
    strict = row > col
    items = list(range(2 * group))
    kh = both(first, k, k2, group, width)
    rk = each(inverse_factor, kh)
    kn = each(lambda x, r: x * r, kh, rk)
    fs = [split(f[n // 2, n % 2]) for n in items]
    b = both_strengths(step, place, first, beta, beta2, group, heads)
    ends = each(split, [leaving[h] for h in range(group)])
    y = [b[n] * (yp[n // 2, n % 2] + mm(xk[n // 2, n % 2], ends[n // 2], NT)) for n in items]
    hand_out(first, y, gv_own, gv_other, width)
    ys = each(split, y)
    e = [jnp.where(strict, mm(ys[n], fs[n], NT), 0.0) for n in items]
    hs = []
    for h in range(group):
        hs += [mm(ends[h], late[h], NN) + g_late[h], ends[h]]
    ts = [(mid if n % 2 else state)[n // 2] for n in items]
    dk = [dkp[n // 2, n % 2] + mm(fs[n], hs[n], NN) - mm(ys[n], ts[n], NN) for n in items]
    rows = [as_row(rk[n], row == col) for n in items]
    dk = [dk[n] - mm((e[n] + e[n].T) * rows[n], exact(kh[n]), NN) for n in items]
    hand_out(first, each(normal_pull, rk, kn, dk), gk_own, gk_other, width)


def params(products):
    return dict(
        compiler_params=pltpu.CompilerParams(vmem_limit_bytes=VMEM_BYTES),
        cost_estimate=pl.CostEstimate(flops=products * 400000000, bytes_accessed=1 << 20, transcendentals=0),
    )


def call_once(body, place, outs, operands, products):
    def whole(array):
        return pl.BlockSpec(array.shape, lambda i, c: (0,) * array.ndim)

    def shaped(shape, dtype, *held):
        return pltpu.HBM(shape, dtype) if held else jax.ShapeDtypeStruct(shape, dtype)

    arrays = [pltpu.with_memory_space_constraint(x, pltpu.HBM) if held else x for x, *held in operands]
    shapes = [shaped(*out) for out in outs]
    return pl.pallas_call(
        body,
        grid_spec=pltpu.PrefetchScalarGridSpec(
            num_scalar_prefetch=1,
            grid=(1,),
            in_specs=[whole(array) for array in arrays],
            out_specs=[whole(jax.ShapeDtypeStruct(shape, dtype)) for shape, dtype, *_ in outs],
        ),
        out_shape=shapes,
        **params(products),
    )(place, *arrays)


def call(body, place, heads, outs, operands, scratch=(), products=1):
    group, steps = heads, 1
    kinds = [kind for kind, _ in operands] + [kind for kind, _, _ in outs] + ["w"] * len(scratch)

    def view(kind, ref, step):
        if kind == "w":
            return ref
        if kind == "h":
            return ref.at[pl.ds(step * group, group)]
        columns = ref.shape[1]
        if kind == "b":
            return ref.at[:, columns - 128 :]
        if isinstance(kind, int):
            wide = 128 * group
            return ref.at[:, pl.ds(pl.multiple_of((kind * steps + step) * wide, wide), wide)]
        return ref.at[:, kind[0] : kind[1]]

    def kernel(place, *refs):
        body(0, place, *[view(kind, ref, 0) for kind, ref in zip(kinds, refs)])

    spec = pl.BlockSpec(memory_space=pltpu.VMEM)
    return pl.pallas_call(
        kernel,
        in_specs=[pl.BlockSpec(memory_space=pltpu.SMEM)] + [spec] * len(operands),
        out_specs=[spec] * len(outs),
        out_shape=[jax.ShapeDtypeStruct(shape, dtype) for _, shape, dtype in outs],
        scratch_shapes=list(scratch),
        **params(products),
    )(place, *[array for _, array in operands])


def run_scan(reverse, place, maps, offsets, shape):
    steps = lax.axis_size("chip")
    share, rows, width = shape
    spec = pl.BlockSpec(memory_space=pltpu.VMEM)
    return pl.pallas_call(
        functools.partial(scan_kernel, reverse, steps, len(maps)),
        in_specs=[pl.BlockSpec(memory_space=pltpu.SMEM)] + [spec] * (len(maps) + len(offsets)),
        out_specs=[spec] * steps,
        out_shape=[jax.ShapeDtypeStruct(shape, f32)] * steps,
        scratch_shapes=[
            pltpu.VMEM((steps, share, width + rows, width), f32),
            pltpu.VMEM((steps,) + shape, f32),
            pltpu.VMEM((steps,) + shape, f32),
        ],
        **params(1),
    )(place, *maps, *offsets)


def swapped(x, axes, distance):
    return lax.ppermute(x, axes, [(i, i ^ distance) for i in range(lax.axis_size(axes))])


def along_chips(pieces):
    came = {0: pieces[0]}
    for d in sorted(range(1, len(pieces)), key=lambda d: -d.bit_count()):
        came[d] = swapped(pieces[d], "chip", d)
    return [came[d] for d in range(len(pieces))]


def to_other_core(x):
    return lax.ppermute(x, "core", [(0, 1), (1, 0)])


def sum_with(x, fillers, place, scale):
    done = []

    def beside(came):
        if len(done) < len(fillers):
            came, outs = lax.optimization_barrier((came, fillers[len(done)](*done)))
            done.append(outs)
        return came

    chips, sequences = lax.axis_size("chip"), lax.axis_size("dp")
    base = 1
    while base < chips:
        x = add_in_pairs([x] + beside([swapped(x, "chip", d) for d in range(base, min(4 * base, chips), base)]))
        base *= 4
    distance = 1
    while distance < sequences:
        x = add_in_pairs([x] + beside([swapped(x, "dp", distance)]))
        distance *= 2
    came = [to_other_core(x)]
    for filler in fillers[len(done) :]:
        done.append(filler(*done))
    spec = pl.BlockSpec(memory_space=pltpu.VMEM)
    out = pl.pallas_call(
        functools.partial(spread_kernel, scale),
        in_specs=[pl.BlockSpec(memory_space=pltpu.SMEM)] + [spec] * (len(came) + 1),
        out_specs=spec,
        out_shape=jax.ShapeDtypeStruct((2 * x.shape[0], x.shape[1]), f32),
        **params(1),
    )(place, x, *came)
    return out.T, done


def shards(queries, keys_in, values_in, inputs, target, gate_weight, beta_bias):
    q, k, v, u, goal = queries[0], keys_in[0], values_in[0], inputs[0], target[0]
    length, model = q.shape
    all_heads = gate_weight.shape[1]
    width = model // all_heads
    heads = all_heads // 2
    half = heads * width
    places = lax.axis_size("chip")
    share = max(1, heads // places)
    copies = max(1, places // heads)
    rows = width // copies
    core = lax.axis_index("core")
    place = jnp.stack([core, lax.axis_index("chip")]).astype(jnp.int32)
    state_shape = (heads, width, width)
    square = (heads, 2, length, width)
    token_half = (length, half)
    stages = 2 if share % 2 == 0 else 1
    whole_shape = (share, rows, width)
    piece_shape = (share // stages, rows, width)
    ordered = pltpu.VMEM((places, share, rows, width), f32)
    squares = ("h", square, f32)
    states = ("h", state_shape, f32)
    halves = (0, token_half, f32)

    def by_stage(pieces):
        return [pieces[stage * places : (stage + 1) * places] for stage in range(stages)]

    with jax.named_scope("to_other_core"):
        beta, send, k_own, v_own = call_once(
            pack_kernel, place,
            [((length, all_heads), f32), ((length, 2 * half + 128), f32), (token_half, f32), (token_half, f32)],
            [(u, HELD), (gate_weight.T, HELD), (beta_bias[None], HELD), (k, HELD), (v, HELD)],
            1,
        )
        early = to_other_core(send)
    with jax.named_scope("rest_to_other_core"):
        send, q_own, goal_own, u_own = call_once(
            pack_rest_kernel, place,
            [((length, 2 * half + model), f32), (token_half, f32), (token_half, f32), (u.shape, bf16)],
            [(q, HELD), (goal, HELD), (u, HELD), (beta,)],
            6,
        )
        send, early = lax.optimization_barrier((send, early))
        rest = to_other_core(send)
    keys = [(0, k_own), (0, early)]
    strengths = [("w", beta), ("b", early)]
    with jax.named_scope("chip_maps"):
        early_map, late_map, early_offset, x, wk, wv, *joint = call(
            functools.partial(maps_kernel, heads, share), place, heads,
            [states] * 3 + [squares] * 3 + [("w", (share // stages, width + rows, width), f32)] * (places * stages),
            keys + [(0, v_own), (1, early)] + strengths,
            products=16,
        )
    with jax.named_scope("maps_to_owners"):
        joint, rest = lax.optimization_barrier((joint, rest))
        maps = [along_chips(part) for part in by_stage(joint)]
    with jax.named_scope("query_terms"):
        p, qt_late, qj, oj = call(
            queries_kernel, place, heads,
            [squares, states] + [squares] * 2,
            [(0, q_own), (0, rest)] + keys + [("h", wk), ("h", wv), ("h", early_map), ("h", early_offset)],
            products=4,
        )
    with jax.named_scope("forward_recurrence"):
        received, states_of = [], None
        for part in maps:
            if states_of is not None:
                part = lax.optimization_barrier((part, states_of))[0]
            states_of = run_scan(False, place, part, [], piece_shape)
            received += along_chips(states_of)
    with jax.named_scope("outputs"):
        rounded, state, *g = call(
            functools.partial(output_kernel, heads, share, places * stages), place, heads,
            [("h", square, bf16), states] + [("w", whole_shape, f32)] * places,
            [("h", qj), ("h", oj), (0, goal_own), (1, rest)] + [("w", piece) for piece in received],
            [ordered],
            products=3,
        )
    with jax.named_scope("cotangents_to_owners"):
        g = along_chips(g)
    with jax.named_scope("fresh_terms"):
        mid, f, g_late, yp, xk, do, out_own, out_other = call(
            fresh_kernel, place, heads,
            [states, squares, states] + [squares] * 3 + [halves] * 2,
            [("h", state), ("h", early_map), ("h", early_offset), ("h", late_map), ("h", wk), ("h", wv)]
            + [("h", p), ("h", rounded), (0, goal_own), (1, rest), ("h", qt_late), ("h", x)] + keys,
            products=8,
        )
        g, f = lax.optimization_barrier((g, f))
    with jax.named_scope("query_gradients"):
        gq_own, gq_other, dkp = call(
            query_kernel, place, heads,
            [halves] * 2 + [squares],
            [("h", state), ("h", mid), ("h", f), ("h", do), (0, q_own), (0, rest)] + keys,
            products=6,
        )
        out_other, gq_other = lax.optimization_barrier((out_other, gq_other))
        out_other, gq_other = to_other_core(out_other), to_other_core(gq_other)
    with jax.named_scope("backward_recurrence"):
        received = along_chips(run_scan(True, place, [piece for part in maps for piece in part], g, whole_shape))
    with jax.named_scope("value_gradients"):
        leaving, gw = call(
            functools.partial(value_kernel, heads, places), place, heads,
            [states, ("w", (heads, model), f32)],
            [("h", yp), ("h", xk), ("h", f)] + strengths
            + [("w", u_own), ((model, 2 * model), rest)]
            + [("w", piece) for piece in received],
            [pltpu.VMEM((2, length, heads), f32), ordered],
            products=3,
        )

    def key_gradients():
        return call(
            functools.partial(key_kernel, heads), place, heads,
            [halves] * 4,
            [("h", leaving), ("h", late_map), ("h", g_late), ("h", state), ("h", mid)]
            + [("h", yp), ("h", xk), ("h", f), ("h", dkp)] + strengths + keys,
            products=6,
        )

    def joined(*halves):
        return call_once(
            join_kernel, place, [((length, model), bf16, HELD)] * (len(halves) // 2), [(x,) for x in halves], 20
        )

    with jax.named_scope("weight_and_key_gradients"):
        gw, (_, (out, gq), (gv, gk)) = sum_with(
            gw,
            [
                key_gradients,
                lambda _: joined(out_own, out_other, gq_own, gq_other),
                lambda grads, _: joined(grads[0], to_other_core(grads[1]), grads[2], to_other_core(grads[3])),
            ],
            place,
            1.0 / math.sqrt(length * 2 * places * lax.axis_size("dp")),
        )
    return (out[None], gq[None], gk[None], gv[None], gw)


def solution(mesh):
    seq, dp = mesh.shape["seq"], mesh.shape["dp"]
    cut = jax.sharding.Mesh(mesh.devices.reshape(seq // 2, 2, dp), ("chip", "core", "dp"))
    split_tokens = P("dp", ("chip", "core"), None)
    return jax.shard_map(
        shards,
        mesh=cut,
        in_specs=(split_tokens,) * 5 + (P(), P()),
        out_specs=(split_tokens,) * 4 + (P(),),
        check_vma=False,
    )
```

time: 613 us -> 80.3 us (0.13)
  waiting for transfers between devices: 283 us -> 9.49 us
  other arithmetic: 168 us -> 0.11 us
  matrix products: 104 us -> 0 us
  local copies, waits for them, and re-layouts: 39.5 us -> 0 us
  starting transfers between devices: 0.2 us -> 35.4 us
  Pallas kernels: 0 us -> 34.3 us
  between operations: 14.7 us -> 0.83 us
    all_gather x4 -> x0, waiting for transfers between devices: 163 us -> none  [carried_in(): pieces = jax.tree.map(lambda part: lax.all_gather(part, axis), value)]
    another operation x3 -> x1, other arithmetic: 161 us -> 0.08 us  [shards(): place = jnp.stack([core, lax.axis_index('chip')]).astype(jnp.int32)]
    psum x1 -> x0, waiting for transfers between devices: 119 us -> none  [shards(): weight_total = lax.psum(local_weight, ('seq', 'dp'))]
    dot_general x37 -> x0, matrix products: 97.4 us -> none  [the longest x14 46.6 us: apply_map(): jnp.einsum('hij,hjk->hik', matrix, carried_state, precision=highest_preci...]
    ppermute x0 -> x30, starting transfers between devices: none -> 35.4 us  [the longest x23 33.4 us: swapped(): lax.ppermute(x, axes, [(i, i ^ distance) for i in range(lax.axis_size(axe...]
    pallas_call x0 -> x15, Pallas kernels: none -> 34.3 us  [the longest x7 22.3 us: call(): pl.pallas_call(kernel, in_specs=[pl.BlockSpec(memory_space=pltpu.SMEM)] +...]
    rev x2 -> x0, local copies, waits for them, and re-layouts: 15.5 us -> none  [carried_in(): pieces = jax.tree.map(lambda part: part[::-1], pieces)]
    ppermute x0 -> x30, waiting for transfers between devices: none -> 9.49 us  [the longest x23 7.99 us: swapped(): lax.ppermute(x, axes, [(i, i ^ distance) for i in range(lax.axis_size(axe...]
  transfers between devices with their start and end apart: 5 -> 30, of which waited for: 5 -> 12; matrix products, arithmetic and copies ran while one was open for 11% -> 0% of each run, Pallas kernels for 0% -> 34%
where the time goes in v1:
time: 80.3 us; the launch traced here: 80.1 us
  starting transfers between devices  35.4 us (44%)
  Pallas kernels  34.3 us (43%)
  waiting for transfers between devices  9.49 us (12%)
  between operations  0.83 us (1%)
    ppermute x23, starting transfers between devices, swapped(): lax.ppermute(x, axes, [(i, i ^ distance) for i in range(lax.axis_size(axe...  33.4 us
    pallas_call x7, Pallas kernels, call(): pl.pallas_call(kernel, in_specs=[pl.BlockSpec(memory_space=pltpu.SMEM)] +...  22.3 us
    ppermute x23, waiting for transfers between devices, swapped(): lax.ppermute(x, axes, [(i, i ^ distance) for i in range(lax.axis_size(axe...  7.99 us
    pallas_call x4, Pallas kernels, call_once(): pl.pallas_call(body, grid_spec=pltpu.PrefetchScalarGridSpec(num_scalar_pr...  7.94 us
    pallas_call x3, Pallas kernels, run_scan(): pl.pallas_call(functools.partial(scan_kernel, reverse, steps, len(maps)),...  2.86 us
    ppermute x7, starting transfers between devices, to_other_core(): return lax.ppermute(x, 'core', [(0, 1), (1, 0)])  2.04 us
  transfers between devices with their start and end apart: 30, of which 12 were waited for; matrix products, arithmetic and copies ran while one was open for 0% of the time, Pallas kernels for 34%

profile of v1, /device:TPU:0, one launch (start us, length us, event | category | flops | bytes accessed | tf_op | source)
XLA Modules:
  0.0 80.1 jit_solution(13801493772286047217)
XLA Ops:
  0.6 0.1 pad_add_fusion.place
  0.7 2.4 %to_other_core.1 = (f32[128,16]{1,0:T(8,128)S(1)}, f32[128,2176]{1,0:T(8,128)S(1)}, f32[128,1024]{1,0:T(8,128)S(1)}, f32[128,1024]{1,0:T(8,128)S(1)}) custom-call(s32[2]{0:T(128)S(1)} %pad_add_fusion.place, bf16[128,2048]{1,0:T(8,128)(2,1)} %bitcast.16, bf16[16,2048]{1,0:T(8,128)(2,1)} %bitcast.18, f32[1,16]{1,0:T(1,128)} %bitcast.19, ...), custom_call_target="tpu_custom_call" | custom-call | flops 400000000 | bytes 1048576 | tf_op jit(solution)/shard_map/to_other_core/pallas_call | solution.py:471
  3.1 0.5 collective-permute-start
  3.6 2.1 %rest_to_other_core.1 = (f32[128,4096]{1,0:T(8,128)S(1)}, f32[128,1024]{1,0:T(8,128)S(1)}, f32[128,1024]{1,0:T(8,128)S(1)}, bf16[128,2048]{1,0:T(8,128)(2,1)S(1)}) custom-call(s32[2]{0:T(128)S(1)} %pad_add_fusion.place, bf16[128,2048]{1,0:T(8,128)(2,1)} %bitcast.20, bf16[128,2048]{1,0:T(8,128)(2,1)} %bitcast.21, bf16[128,2048]{1,0:T(8,128)(2,1)} %bitcast.17, ...), custom_call_target="tpu_custom_call" | custom-call | flops 2400000000 | bytes 1048576 | tf_op jit(solution)/shard_map/rest_to_other_core/pallas_call | solution.py:471
  5.7 0.2 collective-permute-done.refs_1_.refs_3_.refs_5_.refs_13_.refs_4_.refs_7_.refs_10_.refs_12_
  6.0 0.4 collective-permute-start.1
  6.4 5.9 %chip_maps.1 = (f32[8,128,128]{2,1,0:T(8,128)S(1)}, f32[8,128,128]{2,1,0:T(8,128)S(1)}, f32[8,128,128]{2,1,0:T(8,128)S(1)}, f32[8,2,128,128]{3,2,1,0:T(8,128)S(1...) custom-call(s32[2]{0:T(128)S(1)} %pad_add_fusion.place, ...), custom_call_target="tpu_custom_call" | custom-call | flops 6400000000 | bytes 1048576 | tf_op jit(solution)/shard_map/chip_maps/pallas_call | solution.py:505
  12.2 0.0 collective-permute-done.1.refs_1_.refs_3_.refs_9_.refs_6_.refs_5_
  12.2 2.7 %collective-permute-start.2 = (f32[1,256,128]{2,1,0:T(8,128)S(1)}, f32[1,256,128]{2,1,0:T(8,128)S(1)}, u32[]{:S(2)}, u32[]{:S(2)}) collective-permute-start(f32[1,256,128]{2,1,0:T(8,128)S(1)} %get-tuple-element.130), channel_id=1, source_target_pairs={{0,8},{8,0},{16,24},{24,16},{1,9},{9,1},{17,25},{25,17},{2,10},{10... | collective-permute-start | bytes 393224 | tf_op jit(solution)/shard_map/maps_to_owners/ppermute | solution.py:534
  14.9 1.5 %collective-permute-start.3 = (f32[1,256,128]{2,1,0:T(8,128)S(1)}, f32[1,256,128]{2,1,0:T(8,128)S(1)}, u32[]{:S(2)}, u32[]{:S(2)}) collective-permute-start(f32[1,256,128]{2,1,0:T(8,128)S(1)} %get-tuple-element.131), channel_id=1, source_target_pairs={{0,16},{8,24},{16,0},{24,8},{1,17},{9,25},{17,1},{25,9},{2,18},{10... | collective-permute-start | bytes 393224 | tf_op jit(solution)/shard_map/maps_to_owners/ppermute | solution.py:534
  16.5 0.0 collective-permute-start.4
  16.5 1.9 %collective-permute-start.8 = (f32[1,256,128]{2,1,0:T(8,128)S(1)}, f32[1,256,128]{2,1,0:T(8,128)S(1)}, u32[]{:S(2)}, u32[]{:S(2)}) collective-permute-start(f32[1,256,128]{2,1,0:T(8,128)S(1)} %get-tuple-element.138), channel_id=1, source_target_pairs={{0,8},{8,0},{16,24},{24,16},{1,9},{9,1},{17,25},{25,17},{2,10},{10... | collective-permute-start | bytes 393224 | tf_op jit(solution)/shard_map/maps_to_owners/ppermute | solution.py:534
  18.4 1.5 %collective-permute-start.9 = (f32[1,256,128]{2,1,0:T(8,128)S(1)}, f32[1,256,128]{2,1,0:T(8,128)S(1)}, u32[]{:S(2)}, u32[]{:S(2)}) collective-permute-start(f32[1,256,128]{2,1,0:T(8,128)S(1)} %get-tuple-element.139), channel_id=1, source_target_pairs={{0,16},{8,24},{16,0},{24,8},{1,17},{9,25},{17,1},{25,9},{2,18},{10... | collective-permute-start | bytes 393224 | tf_op jit(solution)/shard_map/maps_to_owners/ppermute | solution.py:534
  20.0 2.3 %collective-permute-start.10 = (f32[1,256,128]{2,1,0:T(8,128)S(1)}, f32[1,256,128]{2,1,0:T(8,128)S(1)}, u32[]{:S(2)}, u32[]{:S(2)}) collective-permute-start(f32[1,256,128]{2,1,0:T(8,128)S(1)} %get-tuple-element.140), channel_id=1, source_target_pairs={{0,24},{8,16},{16,8},{24,0},{1,25},{9,17},{17,9},{25,1},{2,26},{10... | collective-permute-start | bytes 393224 | tf_op jit(solution)/shard_map/maps_to_owners/ppermute | solution.py:534
  22.2 1.1 %collective-permute-done.3.refs_2_ = f32[1,256,128]{2,1,0:T(8,128)S(1)} collective-permute-done((f32[1,256,128]{2,1,0:T(8,128)S(1)}, f32[1,256,128]{2,1,0:T(8,128)S(1)}, u32[]{:S(2)}, u32[]{:S(2)}) %collective-permute-start.3) | collective-permute-done | bytes 131104 | tf_op jit(solution)/shard_map/maps_to_owners/ppermute | solution.py:534
  23.3 0.5 collective-permute-done.4.refs_3_
  23.8 0.9 %forward_recurrence.2 = (f32[1,128,128]{2,1,0:T(8,128)S(1)}, f32[1,128,128]{2,1,0:T(8,128)S(1)}, f32[1,128,128]{2,1,0:T(8,128)S(1)}, f32[1,128,128]{2,1,0:T(8,128)S(1)}) custom-call(s32[2]{0:T(128)S(1)} %pad_add_fusion.place, f32[1,256,128]{2,1,0:T(8,128)S(1)} %get-tuple-element.129.refs_0_, f32[1,256,128]{2,1,0:T(8,128)S(1)} %collective-permute-done.2.refs_1_, ...), custom_call_target="tpu_custom_call" | custom-call | flops 400000000 | bytes 1048576 | tf_op jit(solution)/shard_map/forward_recurrence/pallas_call | solution.py:519
  24.7 1.3 %collective-permute-start.5 = (f32[1,128,128]{2,1,0:T(8,128)S(1)}, f32[1,128,128]{2,1,0:T(8,128)S(1)}, u32[]{:S(2)}, u32[]{:S(2)}) collective-permute-start(f32[1,128,128]{2,1,0:T(8,128)S(1)} %get-tuple-element.134), channel_id=1, source_target_pairs={{0,8},{8,0},{16,24},{24,16},{1,9},{9,1},{17,25},{25,17},{2,10},{10... | collective-permute-start | bytes 196616 | tf_op jit(solution)/shard_map/forward_recurrence/ppermute | solution.py:534
  26.1 1.2 %collective-permute-start.6 = (f32[1,128,128]{2,1,0:T(8,128)S(1)}, f32[1,128,128]{2,1,0:T(8,128)S(1)}, u32[]{:S(2)}, u32[]{:S(2)}) collective-permute-start(f32[1,128,128]{2,1,0:T(8,128)S(1)} %get-tuple-element.135), channel_id=1, source_target_pairs={{0,16},{8,24},{16,0},{24,8},{1,17},{9,25},{17,1},{25,9},{2,18},{10... | collective-permute-start | bytes 196616 | tf_op jit(solution)/shard_map/forward_recurrence/ppermute | solution.py:534
  27.3 0.0 collective-permute-done.8.refs_1_.refs_5_
  27.3 1.4 %collective-permute-start.7 = (f32[1,128,128]{2,1,0:T(8,128)S(1)}, f32[1,128,128]{2,1,0:T(8,128)S(1)}, u32[]{:S(2)}, u32[]{:S(2)}) collective-permute-start(f32[1,128,128]{2,1,0:T(8,128)S(1)} %get-tuple-element.136), channel_id=1, source_target_pairs={{0,24},{8,16},{16,8},{24,0},{1,25},{9,17},{17,9},{25,1},{2,26},{10... | collective-permute-start | bytes 196616 | tf_op jit(solution)/shard_map/forward_recurrence/ppermute | solution.py:534
  28.7 0.7 collective-permute-done.9.refs_2_.refs_6_
  29.3 0.2 collective-permute-done.10.refs_3_.refs_7_
  29.5 0.9 %forward_recurrence.3 = (f32[1,128,128]{2,1,0:T(8,128)S(1)}, f32[1,128,128]{2,1,0:T(8,128)S(1)}, f32[1,128,128]{2,1,0:T(8,128)S(1)}, f32[1,128,128]{2,1,0:T(8,128)S(1)}) custom-call(s32[2]{0:T(128)S(1)} %pad_add_fusion.place, f32[1,256,128]{2,1,0:T(8,128)S(1)} %get-tuple-element.141.refs_0_.refs_4_, ...), custom_call_target="tpu_custom_call" | custom-call | flops 400000000 | bytes 1048576 | tf_op jit(solution)/shard_map/forward_recurrence/pallas_call | solution.py:519
  30.4 1.3 %collective-permute-start.11 = (f32[1,128,128]{2,1,0:T(8,128)S(1)}, f32[1,128,128]{2,1,0:T(8,128)S(1)}, u32[]{:S(2)}, u32[]{:S(2)}) collective-permute-start(f32[1,128,128]{2,1,0:T(8,128)S(1)} %get-tuple-element.146), channel_id=1, source_target_pairs={{0,8},{8,0},{16,24},{24,16},{1,9},{9,1},{17,25},{25,17},{2,10},{10... | collective-permute-start | bytes 196616 | tf_op jit(solution)/shard_map/forward_recurrence/ppermute | solution.py:534
  31.7 1.1 %collective-permute-start.12 = (f32[1,128,128]{2,1,0:T(8,128)S(1)}, f32[1,128,128]{2,1,0:T(8,128)S(1)}, u32[]{:S(2)}, u32[]{:S(2)}) collective-permute-start(f32[1,128,128]{2,1,0:T(8,128)S(1)} %get-tuple-element.147), channel_id=1, source_target_pairs={{0,16},{8,24},{16,0},{24,8},{1,17},{9,25},{17,1},{25,9},{2,18},{10... | collective-permute-start | bytes 196616 | tf_op jit(solution)/shard_map/forward_recurrence/ppermute | solution.py:534
  32.9 0.0 collective-permute-done.5.refs_5_
  32.9 1.4 %collective-permute-start.13 = (f32[1,128,128]{2,1,0:T(8,128)S(1)}, f32[1,128,128]{2,1,0:T(8,128)S(1)}, u32[]{:S(2)}, u32[]{:S(2)}) collective-permute-start(f32[1,128,128]{2,1,0:T(8,128)S(1)} %get-tuple-element.148), channel_id=1, source_target_pairs={{0,24},{8,16},{16,8},{24,0},{1,25},{9,17},{17,9},{25,1},{2,26},{10... | collective-permute-start | bytes 196616 | tf_op jit(solution)/shard_map/forward_recurrence/ppermute | solution.py:534
  34.3 2.6 %query_terms.1 = (f32[8,2,128,128]{3,2,1,0:T(8,128)S(1)}, f32[8,128,128]{2,1,0:T(8,128)S(1)}, f32[8,2,128,128]{3,2,1,0:T(8,128)S(1)}, f32[8,2,128,128]{3,2,1,0:T(8,128)S(1)}) custom-call(s32[2]{0:T(128)S(1)} %pad_add_fusion.place, f32[128,1024]{1,0:T(8,128)S(1)} %get-tuple-element.106.refs_0_.refs_4_, ...), custom_call_target="tpu_custom_call" | custom-call | flops 1600000000 | bytes 1048576 | tf_op jit(solution)/shard_map/query_terms/pallas_call | solution.py:505
  36.9 0.0 collective-permute-done.7.refs_7_
  36.9 0.0 collective-permute-done.11.refs_9_
  36.9 1.1 %collective-permute-done.13.refs_11_ = f32[1,128,128]{2,1,0:T(8,128)S(1)} collective-permute-done((f32[1,128,128]{2,1,0:T(8,128)S(1)}, f32[1,128,128]{2,1,0:T(8,128)S(1)}, u32[]{:S(2)}, u32[]{:S(2)}) %collective-permute-start.13) | collective-permute-done | bytes 65568 | tf_op jit(solution)/shard_map/forward_recurrence/ppermute | solution.py:534
  38.0 2.1 %outputs.1 = (bf16[8,2,128,128]{3,2,1,0:T(8,128)(2,1)S(1)}, f32[8,128,128]{2,1,0:T(8,128)S(1)}, f32[2,128,128]{2,1,0:T(8,128)S(1)}, f32[2,128,128]{2,1,0:T(8,128...) custom-call(s32[2]{0:T(128)S(1)} %pad_add_fusion.place, ...), custom_call_target="tpu_custom_call" | custom-call | flops 1200000000 | bytes 1048576 | tf_op jit(solution)/shard_map/outputs/pallas_call | solution.py:505
  40.2 2.0 %collective-permute-start.14 = (f32[2,128,128]{2,1,0:T(8,128)S(1)}, f32[2,128,128]{2,1,0:T(8,128)S(1)}, u32[]{:S(2)}, u32[]{:S(2)}) collective-permute-start(f32[2,128,128]{2,1,0:T(8,128)S(1)} %get-tuple-element.158), channel_id=1, source_target_pairs={{0,8},{8,0},{16,24},{24,16},{1,9},{9,1},{17,25},{25,17},{2,10},{10... | collective-permute-start | bytes 393224 | tf_op jit(solution)/shard_map/cotangents_to_owners/ppermute | solution.py:534
  42.2 0.0 collective-permute-start.15
  42.2 1.5 %collective-permute-start.16 = (f32[2,128,128]{2,1,0:T(8,128)S(1)}, f32[2,128,128]{2,1,0:T(8,128)S(1)}, u32[]{:S(2)}, u32[]{:S(2)}) collective-permute-start(f32[2,128,128]{2,1,0:T(8,128)S(1)} %get-tuple-element.160), channel_id=1, source_target_pairs={{0,24},{8,16},{16,8},{24,0},{1,25},{9,17},{17,9},{25,1},{2,26},{10... | collective-permute-start | bytes 393224 | tf_op jit(solution)/shard_map/cotangents_to_owners/ppermute | solution.py:534
  43.7 3.4 %fresh_terms.1 = (f32[8,128,128]{2,1,0:T(8,128)S(1)}, f32[8,2,128,128]{3,2,1,0:T(8,128)S(1)}, f32[8,128,128]{2,1,0:T(8,128)S(1)}, f32[8,2,128,128]{3,2,1,0:T(8,1...) custom-call(s32[2]{0:T(128)S(1)} %pad_add_fusion.place, ...), custom_call_target="tpu_custom_call" | custom-call | flops 3200000000 | bytes 1048576 | tf_op jit(solution)/shard_map/fresh_terms/pallas_call | solution.py:505
  47.2 1.4 %collective-permute-done.15.refs_10_ = f32[2,128,128]{2,1,0:T(8,128)S(1)} collective-permute-done((f32[2,128,128]{2,1,0:T(8,128)S(1)}, f32[2,128,128]{2,1,0:T(8,128)S(1)}, u32[]{:S(2)}, u32[]{:S(2)}) %collective-permute-start.15) | collective-permute-done | bytes 131104 | tf_op jit(solution)/shard_map/cotangents_to_owners/ppermute | solution.py:534
  48.6 1.0 %backward_recurrence.1 = (f32[2,128,128]{2,1,0:T(8,128)S(1)}, f32[2,128,128]{2,1,0:T(8,128)S(1)}, f32[2,128,128]{2,1,0:T(8,128)S(1)}, f32[2,128,128]{2,1,0:T(8,128)S(1)}) custom-call(s32[2]{0:T(128)S(1)} %pad_add_fusion.place, f32[1,256,128]{2,1,0:T(8,128)S(1)} %get-tuple-element.129.refs_0_, f32[1,256,128]{2,1,0:T(8,128)S(1)} %collective-permute-done.2.refs_1_, ...), custom_call_target="tpu_custom_call" | custom-call | flops 400000000 | bytes 1048576 | tf_op jit(solution)/shard_map/backward_recurrence/pallas_call | solution.py:519
  49.6 0.9 %collective-permute-start.17 = (f32[2,128,128]{2,1,0:T(8,128)S(1)}, f32[2,128,128]{2,1,0:T(8,128)S(1)}, u32[]{:S(2)}, u32[]{:S(2)}) collective-permute-start(f32[2,128,128]{2,1,0:T(8,128)S(1)} %get-tuple-element.169), channel_id=1, source_target_pairs={{0,8},{8,0},{16,24},{24,16},{1,9},{9,1},{17,25},{25,17},{2,10},{10... | collective-permute-start | bytes 393224 | tf_op jit(solution)/shard_map/backward_recurrence/ppermute | solution.py:534
  50.5 2.0 %collective-permute-start.18 = (f32[2,128,128]{2,1,0:T(8,128)S(1)}, f32[2,128,128]{2,1,0:T(8,128)S(1)}, u32[]{:S(2)}, u32[]{:S(2)}) collective-permute-start(f32[2,128,128]{2,1,0:T(8,128)S(1)} %get-tuple-element.170), channel_id=1, source_target_pairs={{0,16},{8,24},{16,0},{24,8},{1,17},{9,25},{17,1},{25,9},{2,18},{10... | collective-permute-start | bytes 393224 | tf_op jit(solution)/shard_map/backward_recurrence/ppermute | solution.py:534
  52.5 1.4 %collective-permute-start.19 = (f32[2,128,128]{2,1,0:T(8,128)S(1)}, f32[2,128,128]{2,1,0:T(8,128)S(1)}, u32[]{:S(2)}, u32[]{:S(2)}) collective-permute-start(f32[2,128,128]{2,1,0:T(8,128)S(1)} %get-tuple-element.171), channel_id=1, source_target_pairs={{0,24},{8,16},{16,8},{24,0},{1,25},{9,17},{17,9},{25,1},{2,26},{10... | collective-permute-start | bytes 393224 | tf_op jit(solution)/shard_map/backward_recurrence/ppermute | solution.py:534
  53.9 2.7 %query_gradients.1 = (f32[128,1024]{1,0:T(8,128)S(1)}, f32[128,1024]{1,0:T(8,128)S(1)}, f32[8,2,128,128]{3,2,1,0:T(8,128)S(1)}) custom-call(s32[2]{0:T(128)S(1)} %pad_add_fusion.place, f32[8,128,128]{2,1,0:T(8,128)S(1)} %get-tuple-element.149.refs_0_.refs_3_, f32[8,128,128]{2,1,0:T(8,128)S(1)} %get-tuple-element.175.refs_1_.refs_4_, ...), custom_call_target="tpu_custom_call" | custom-call | flops 2400000000 | bytes 1048576 | tf_op jit(solution)/shard_map/query_gradients/pallas_call | solution.py:505
  56.6 0.1 collective-permute-start.24
  56.6 0.5 collective-permute-start.25
  57.1 0.0 collective-permute-done.17.refs_8_
  57.1 0.0 collective-permute-done.18.refs_9_
  57.1 1.2 %collective-permute-done.19.refs_10_ = f32[2,128,128]{2,1,0:T(8,128)S(1)} collective-permute-done((f32[2,128,128]{2,1,0:T(8,128)S(1)}, f32[2,128,128]{2,1,0:T(8,128)S(1)}, u32[]{:S(2)}, u32[]{:S(2)}) %collective-permute-start.19) | collective-permute-done | bytes 131104 | tf_op jit(solution)/shard_map/backward_recurrence/ppermute | solution.py:534
  58.3 2.0 %value_gradients.1 = (f32[8,128,128]{2,1,0:T(8,128)S(1)}, f32[8,2048]{1,0:T(8,128)S(1)}) custom-call(s32[2]{0:T(128)S(1)} %pad_add_fusion.place, f32[8,2,128,128]{3,2,1,0:T(8,128)S(1)} %get-tuple-element.155.refs_0_.refs_5_, f32[8,2,128,128]{3,2,1,0:T(8,128)S(1)} %get-tuple-element.156.refs_1_.refs_6_, ...), custom_call_target="tpu_custom_call" | custom-call | flops 1200000000 | bytes 1048576 | tf_op jit(solution)/shard_map/value_gradients/pallas_call | solution.py:505
  60.3 1.9 %collective-permute-start.22 = (f32[8,2048]{1,0:T(8,128)S(1)}, f32[8,2048]{1,0:T(8,128)S(1)}, u32[]{:S(2)}, u32[]{:S(2)}) collective-permute-start(f32[8,2048]{1,0:T(8,128)S(1)} %get-tuple-element.172), channel_id=1, source_target_pairs={{0,24},{8,16},{16,8},{24,0},{1,25},{9,17},{17,9},{25,1},{2,26},{10... | collective-permute-start | bytes 196616 | tf_op jit(solution)/shard_map/weight_and_key_gradients/ppermute | solution.py:534
  62.2 1.5 %collective-permute-start.21 = (f32[8,2048]{1,0:T(8,128)S(1)}, f32[8,2048]{1,0:T(8,128)S(1)}, u32[]{:S(2)}, u32[]{:S(2)}) collective-permute-start(f32[8,2048]{1,0:T(8,128)S(1)} %get-tuple-element.172), channel_id=1, source_target_pairs={{0,16},{8,24},{16,0},{24,8},{1,17},{9,25},{17,1},{25,9},{2,18},{10... | collective-permute-start | bytes 196616 | tf_op jit(solution)/shard_map/weight_and_key_gradients/ppermute | solution.py:534
  63.7 0.1 collective-permute-start.20
  63.8 3.6 %weight_and_key_gradients.4 = (f32[128,1024]{1,0:T(8,128)S(1)}, f32[128,1024]{1,0:T(8,128)S(1)}, f32[128,1024]{1,0:T(8,128)S(1)}, f32[128,1024]{1,0:T(8,128)S(1)}) custom-call(s32[2]{0:T(128)S(1)} %pad_add_fusion.place, f32[8,128,128]{2,1,0:T(8,128)S(1)} %get-tuple-element.173.refs_0_, f32[8,128,128]{2,1,0:T(8,128)S(1)} %get-tuple-element.150.refs_3_.refs_1_, ...), custom_call_target="tpu_custom_call" | custom-call | flops 2400000000 | bytes 1048576 | tf_op jit(solution)/shard_map/weight_and_key_gradients/pallas_call | solution.py:505
  67.4 0.5 collective-permute-done.20
  68.0 1.7 %collective-permute-start.23 = (f32[8,2048]{1,0:T(8,128)S(1)}, f32[8,2048]{1,0:T(8,128)S(1)}, u32[]{:S(2)}, u32[]{:S(2)}) collective-permute-start(f32[8,2048]{1,0:T(8,128)S(1)} %add_add_fusion), channel_id=1, source_target_pairs={{0,1},{1,0},{2,3},{3,2},{4,5},{5,4},{6,7},{7,6},{8,9},{9,8},{10,11... | collective-permute-start | bytes 196616 | tf_op jit(solution)/shard_map/weight_and_key_gradients/ppermute | solution.py:534
  69.7 0.5 collective-permute-start.28
  70.2 1.7 %weight_and_key_gradients.5 = (bf16[128,2048]{1,0:T(8,128)(2,1)}, bf16[128,2048]{1,0:T(8,128)(2,1)}) custom-call(s32[2]{0:T(128)S(1)} %pad_add_fusion.place, f32[128,1024]{1,0:T(8,128)S(1)} %get-tuple-element.185.refs_0_, f32[128,1024]{1,0:T(8,128)S(1)} %collective-permute-done.24.refs_1_, f32[128,1024]{1,0:T(8,128)S(1)} %get-tuple-element.189.refs_2_, ...), custom_call_target="tpu_custom_call" | custom-call | flops 8000000000 | bytes 1048576 | tf_op jit(solution)/shard_map/weight_and_key_gradients/pallas_call | solution.py:471
  71.9 0.5 collective-permute-done.23
  72.4 2.7 %collective-permute-start.26 = (f32[8,2048]{1,0:T(8,128)S(1)}, f32[8,2048]{1,0:T(8,128)S(1)}, u32[]{:S(2)}, u32[]{:S(2)}) collective-permute-start(f32[8,2048]{1,0:T(8,128)S(1)} %add.18), channel_id=1, source_target_pairs={{0,2},{1,3},{2,0},{3,1},{4,6},{5,7},{6,4},{7,5},{8,10},{9,11},{10,... | collective-permute-start | bytes 196616 | tf_op jit(solution)/shard_map/weight_and_key_gradients/ppermute | solution.py:534
  75.0 1.7 %weight_and_key_gradients.6 = (bf16[128,2048]{1,0:T(8,128)(2,1)}, bf16[128,2048]{1,0:T(8,128)(2,1)}) custom-call(s32[2]{0:T(128)S(1)} %pad_add_fusion.place, f32[128,1024]{1,0:T(8,128)S(1)} %get-tuple-element.196.refs_0_, f32[128,1024]{1,0:T(8,128)S(1)} %collective-permute-done.27.refs_1_, f32[128,1024]{1,0:T(8,128)S(1)} %get-tuple-element.198.refs_2_, ...), custom_call_target="tpu_custom_call" | custom-call | flops 8000000000 | bytes 1048576 | tf_op jit(solution)/shard_map/weight_and_key_gradients/pallas_call | solution.py:471
  76.8 0.8 %collective-permute-done.26 = f32[8,2048]{1,0:T(8,128)S(1)} collective-permute-done((f32[8,2048]{1,0:T(8,128)S(1)}, f32[8,2048]{1,0:T(8,128)S(1)}, u32[]{:S(2)}, u32[]{:S(2)}) %collective-permute-start.26) | collective-permute-done | bytes 65568 | tf_op jit(solution)/shard_map/weight_and_key_gradients/ppermute | solution.py:534
  77.6 0.1 collective-permute-start.29
  77.7 1.2 %collective-permute-done.29.refs_1_ = f32[8,2048]{1,0:T(8,128)S(1)} collective-permute-done((f32[8,2048]{1,0:T(8,128)S(1)}, f32[8,2048]{1,0:T(8,128)S(1)}, u32[]{:S(2)}, u32[]{:S(2)}) %collective-permute-start.29) | collective-permute-done | bytes 65568 | tf_op jit(solution)/shard_map/weight_and_key_gradients/ppermute | solution.py:545
  78.9 1.2 %weight_and_key_gradients.7 = f32[16,2048]{1,0:T(8,128)} custom-call(s32[2]{0:T(128)S(1)} %pad_add_fusion.place, f32[8,2048]{1,0:T(8,128)S(1)} %add.19.refs_0_, f32[8,2048]{1,0:T(8,128)S(1)} %collective-permute-done.29.refs_1_), custom_call_target="tpu_custom_call" | custom-call | flops 400000000 | bytes 1048576 | tf_op jit(solution)/shard_map/weight_and_key_gradients/pallas_call | solution.py:570
  (15 shorter events, 0.1 us)
Async XLA Ops:
  3.1 2.9 %collective-permute-start = (f32[128,2176]{1,0:T(8,128)S(1)}, f32[128,2176]{1,0:T(8,128)S(1)}, u32[]{:S(2)}, u32[]{:S(2)}) collective-permute-start(f32[128,2176]{1,0:T(8,128)S(1)} %get-tuple-element.109), channel_id=1, source_target_pairs={{0,4},{4,0},{1,5},{5,1},{2,6},{6,2},{3,7},{7,3},{8,12},{12,8},{9,1... | collective-permute-start | bytes 3342344 | tf_op jit(solution)/shard_map/to_other_core/ppermute | solution.py:545
  6.0 6.3 %collective-permute-start.1 = (f32[128,4096]{1,0:T(8,128)S(1)}, f32[128,4096]{1,0:T(8,128)S(1)}, u32[]{:S(2)}, u32[]{:S(2)}) collective-permute-start(f32[128,4096]{1,0:T(8,128)S(1)} %get-tuple-element.120), channel_id=1, source_target_pairs={{0,4},{4,0},{1,5},{5,1},{2,6},{6,2},{3,7},{7,3},{8,12},{12,8},{9,1... | collective-permute-start | bytes 6291464 | tf_op jit(solution)/shard_map/rest_to_other_core/ppermute | solution.py:545
  12.2 7.7 %collective-permute-start.2 = (f32[1,256,128]{2,1,0:T(8,128)S(1)}, f32[1,256,128]{2,1,0:T(8,128)S(1)}, u32[]{:S(2)}, u32[]{:S(2)}) collective-permute-start(f32[1,256,128]{2,1,0:T(8,128)S(1)} %get-tuple-element.130), channel_id=1, source_target_pairs={{0,8},{8,0},{16,24},{24,16},{1,9},{9,1},{17,25},{25,17},{2,10},{10... | collective-permute-start | bytes 393224 | tf_op jit(solution)/shard_map/maps_to_owners/ppermute | solution.py:534
  14.9 8.3 %collective-permute-start.3 = (f32[1,256,128]{2,1,0:T(8,128)S(1)}, f32[1,256,128]{2,1,0:T(8,128)S(1)}, u32[]{:S(2)}, u32[]{:S(2)}) collective-permute-start(f32[1,256,128]{2,1,0:T(8,128)S(1)} %get-tuple-element.131), channel_id=1, source_target_pairs={{0,16},{8,24},{16,0},{24,8},{1,17},{9,25},{17,1},{25,9},{2,18},{10... | collective-permute-start | bytes 393224 | tf_op jit(solution)/shard_map/maps_to_owners/ppermute | solution.py:534
  16.5 7.3 %collective-permute-start.4 = (f32[1,256,128]{2,1,0:T(8,128)S(1)}, f32[1,256,128]{2,1,0:T(8,128)S(1)}, u32[]{:S(2)}, u32[]{:S(2)}) collective-permute-start(f32[1,256,128]{2,1,0:T(8,128)S(1)} %get-tuple-element.132), channel_id=1, source_target_pairs={{0,24},{8,16},{16,8},{24,0},{1,25},{9,17},{17,9},{25,1},{2,26},{10... | collective-permute-start | bytes 393224 | tf_op jit(solution)/shard_map/maps_to_owners/ppermute | solution.py:534
  16.5 10.8 %collective-permute-start.8 = (f32[1,256,128]{2,1,0:T(8,128)S(1)}, f32[1,256,128]{2,1,0:T(8,128)S(1)}, u32[]{:S(2)}, u32[]{:S(2)}) collective-permute-start(f32[1,256,128]{2,1,0:T(8,128)S(1)} %get-tuple-element.138), channel_id=1, source_target_pairs={{0,8},{8,0},{16,24},{24,16},{1,9},{9,1},{17,25},{25,17},{2,10},{10... | collective-permute-start | bytes 393224 | tf_op jit(solution)/shard_map/maps_to_owners/ppermute | solution.py:534
  18.4 10.9 %collective-permute-start.9 = (f32[1,256,128]{2,1,0:T(8,128)S(1)}, f32[1,256,128]{2,1,0:T(8,128)S(1)}, u32[]{:S(2)}, u32[]{:S(2)}) collective-permute-start(f32[1,256,128]{2,1,0:T(8,128)S(1)} %get-tuple-element.139), channel_id=1, source_target_pairs={{0,16},{8,24},{16,0},{24,8},{1,17},{9,25},{17,1},{25,9},{2,18},{10... | collective-permute-start | bytes 393224 | tf_op jit(solution)/shard_map/maps_to_owners/ppermute | solution.py:534
  20.0 9.5 %collective-permute-start.10 = (f32[1,256,128]{2,1,0:T(8,128)S(1)}, f32[1,256,128]{2,1,0:T(8,128)S(1)}, u32[]{:S(2)}, u32[]{:S(2)}) collective-permute-start(f32[1,256,128]{2,1,0:T(8,128)S(1)} %get-tuple-element.140), channel_id=1, source_target_pairs={{0,24},{8,16},{16,8},{24,0},{1,25},{9,17},{17,9},{25,1},{2,26},{10... | collective-permute-start | bytes 393224 | tf_op jit(solution)/shard_map/maps_to_owners/ppermute | solution.py:534
  24.7 8.1 %collective-permute-start.5 = (f32[1,128,128]{2,1,0:T(8,128)S(1)}, f32[1,128,128]{2,1,0:T(8,128)S(1)}, u32[]{:S(2)}, u32[]{:S(2)}) collective-permute-start(f32[1,128,128]{2,1,0:T(8,128)S(1)} %get-tuple-element.134), channel_id=1, source_target_pairs={{0,8},{8,0},{16,24},{24,16},{1,9},{9,1},{17,25},{25,17},{2,10},{10... | collective-permute-start | bytes 196616 | tf_op jit(solution)/shard_map/forward_recurrence/ppermute | solution.py:534
  26.1 10.8 %collective-permute-start.6 = (f32[1,128,128]{2,1,0:T(8,128)S(1)}, f32[1,128,128]{2,1,0:T(8,128)S(1)}, u32[]{:S(2)}, u32[]{:S(2)}) collective-permute-start(f32[1,128,128]{2,1,0:T(8,128)S(1)} %get-tuple-element.135), channel_id=1, source_target_pairs={{0,16},{8,24},{16,0},{24,8},{1,17},{9,25},{17,1},{25,9},{2,18},{10... | collective-permute-start | bytes 196616 | tf_op jit(solution)/shard_map/forward_recurrence/ppermute | solution.py:534
  27.3 9.6 %collective-permute-start.7 = (f32[1,128,128]{2,1,0:T(8,128)S(1)}, f32[1,128,128]{2,1,0:T(8,128)S(1)}, u32[]{:S(2)}, u32[]{:S(2)}) collective-permute-start(f32[1,128,128]{2,1,0:T(8,128)S(1)} %get-tuple-element.136), channel_id=1, source_target_pairs={{0,24},{8,16},{16,8},{24,0},{1,25},{9,17},{17,9},{25,1},{2,26},{10... | collective-permute-start | bytes 196616 | tf_op jit(solution)/shard_map/forward_recurrence/ppermute | solution.py:534
  30.4 6.5 %collective-permute-start.11 = (f32[1,128,128]{2,1,0:T(8,128)S(1)}, f32[1,128,128]{2,1,0:T(8,128)S(1)}, u32[]{:S(2)}, u32[]{:S(2)}) collective-permute-start(f32[1,128,128]{2,1,0:T(8,128)S(1)} %get-tuple-element.146), channel_id=1, source_target_pairs={{0,8},{8,0},{16,24},{24,16},{1,9},{9,1},{17,25},{25,17},{2,10},{10... | collective-permute-start | bytes 196616 | tf_op jit(solution)/shard_map/forward_recurrence/ppermute | solution.py:534
  31.7 5.2 %collective-permute-start.12 = (f32[1,128,128]{2,1,0:T(8,128)S(1)}, f32[1,128,128]{2,1,0:T(8,128)S(1)}, u32[]{:S(2)}, u32[]{:S(2)}) collective-permute-start(f32[1,128,128]{2,1,0:T(8,128)S(1)} %get-tuple-element.147), channel_id=1, source_target_pairs={{0,16},{8,24},{16,0},{24,8},{1,17},{9,25},{17,1},{25,9},{2,18},{10... | collective-permute-start | bytes 196616 | tf_op jit(solution)/shard_map/forward_recurrence/ppermute | solution.py:534
  32.9 5.2 %collective-permute-start.13 = (f32[1,128,128]{2,1,0:T(8,128)S(1)}, f32[1,128,128]{2,1,0:T(8,128)S(1)}, u32[]{:S(2)}, u32[]{:S(2)}) collective-permute-start(f32[1,128,128]{2,1,0:T(8,128)S(1)} %get-tuple-element.148), channel_id=1, source_target_pairs={{0,24},{8,16},{16,8},{24,0},{1,25},{9,17},{17,9},{25,1},{2,26},{10... | collective-permute-start | bytes 196616 | tf_op jit(solution)/shard_map/forward_recurrence/ppermute | solution.py:534
  40.2 7.0 %collective-permute-start.14 = (f32[2,128,128]{2,1,0:T(8,128)S(1)}, f32[2,128,128]{2,1,0:T(8,128)S(1)}, u32[]{:S(2)}, u32[]{:S(2)}) collective-permute-start(f32[2,128,128]{2,1,0:T(8,128)S(1)} %get-tuple-element.158), channel_id=1, source_target_pairs={{0,8},{8,0},{16,24},{24,16},{1,9},{9,1},{17,25},{25,17},{2,10},{10... | collective-permute-start | bytes 393224 | tf_op jit(solution)/shard_map/cotangents_to_owners/ppermute | solution.py:534
  42.2 6.4 %collective-permute-start.15 = (f32[2,128,128]{2,1,0:T(8,128)S(1)}, f32[2,128,128]{2,1,0:T(8,128)S(1)}, u32[]{:S(2)}, u32[]{:S(2)}) collective-permute-start(f32[2,128,128]{2,1,0:T(8,128)S(1)} %get-tuple-element.159), channel_id=1, source_target_pairs={{0,16},{8,24},{16,0},{24,8},{1,17},{9,25},{17,1},{25,9},{2,18},{10... | collective-permute-start | bytes 393224 | tf_op jit(solution)/shard_map/cotangents_to_owners/ppermute | solution.py:534
  42.2 6.4 %collective-permute-start.16 = (f32[2,128,128]{2,1,0:T(8,128)S(1)}, f32[2,128,128]{2,1,0:T(8,128)S(1)}, u32[]{:S(2)}, u32[]{:S(2)}) collective-permute-start(f32[2,128,128]{2,1,0:T(8,128)S(1)} %get-tuple-element.160), channel_id=1, source_target_pairs={{0,24},{8,16},{16,8},{24,0},{1,25},{9,17},{17,9},{25,1},{2,26},{10... | collective-permute-start | bytes 393224 | tf_op jit(solution)/shard_map/cotangents_to_owners/ppermute | solution.py:534
  49.6 7.6 %collective-permute-start.17 = (f32[2,128,128]{2,1,0:T(8,128)S(1)}, f32[2,128,128]{2,1,0:T(8,128)S(1)}, u32[]{:S(2)}, u32[]{:S(2)}) collective-permute-start(f32[2,128,128]{2,1,0:T(8,128)S(1)} %get-tuple-element.169), channel_id=1, source_target_pairs={{0,8},{8,0},{16,24},{24,16},{1,9},{9,1},{17,25},{25,17},{2,10},{10... | collective-permute-start | bytes 393224 | tf_op jit(solution)/shard_map/backward_recurrence/ppermute | solution.py:534
  50.5 6.7 %collective-permute-start.18 = (f32[2,128,128]{2,1,0:T(8,128)S(1)}, f32[2,128,128]{2,1,0:T(8,128)S(1)}, u32[]{:S(2)}, u32[]{:S(2)}) collective-permute-start(f32[2,128,128]{2,1,0:T(8,128)S(1)} %get-tuple-element.170), channel_id=1, source_target_pairs={{0,16},{8,24},{16,0},{24,8},{1,17},{9,25},{17,1},{25,9},{2,18},{10... | collective-permute-start | bytes 393224 | tf_op jit(solution)/shard_map/backward_recurrence/ppermute | solution.py:534
  52.5 5.9 %collective-permute-start.19 = (f32[2,128,128]{2,1,0:T(8,128)S(1)}, f32[2,128,128]{2,1,0:T(8,128)S(1)}, u32[]{:S(2)}, u32[]{:S(2)}) collective-permute-start(f32[2,128,128]{2,1,0:T(8,128)S(1)} %get-tuple-element.171), channel_id=1, source_target_pairs={{0,24},{8,16},{16,8},{24,0},{1,25},{9,17},{17,9},{25,1},{2,26},{10... | collective-permute-start | bytes 393224 | tf_op jit(solution)/shard_map/backward_recurrence/ppermute | solution.py:534
  56.6 13.6 %collective-permute-start.24 = (f32[128,1024]{1,0:T(8,128)S(1)}, f32[128,1024]{1,0:T(8,128)S(1)}, u32[]{:S(2)}, u32[]{:S(2)}) collective-permute-start(f32[128,1024]{1,0:T(8,128)S(1)} %get-tuple-element.188), channel_id=1, source_target_pairs={{0,4},{4,0},{1,5},{5,1},{2,6},{6,2},{3,7},{7,3},{8,12},{12,8},{9,1... | collective-permute-start | bytes 1572872 | tf_op jit(solution)/shard_map/query_gradients/ppermute | solution.py:545
  56.6 13.5 %collective-permute-start.25 = (f32[128,1024]{1,0:T(8,128)S(1)}, f32[128,1024]{1,0:T(8,128)S(1)}, u32[]{:S(2)}, u32[]{:S(2)}) collective-permute-start(f32[128,1024]{1,0:T(8,128)S(1)} %get-tuple-element.190), channel_id=1, source_target_pairs={{0,4},{4,0},{1,5},{5,1},{2,6},{6,2},{3,7},{7,3},{8,12},{12,8},{9,1... | collective-permute-start | bytes 1572872 | tf_op jit(solution)/shard_map/query_gradients/ppermute | solution.py:545
  60.3 7.1 %collective-permute-start.22 = (f32[8,2048]{1,0:T(8,128)S(1)}, f32[8,2048]{1,0:T(8,128)S(1)}, u32[]{:S(2)}, u32[]{:S(2)}) collective-permute-start(f32[8,2048]{1,0:T(8,128)S(1)} %get-tuple-element.172), channel_id=1, source_target_pairs={{0,24},{8,16},{16,8},{24,0},{1,25},{9,17},{17,9},{25,1},{2,26},{10... | collective-permute-start | bytes 196616 | tf_op jit(solution)/shard_map/weight_and_key_gradients/ppermute | solution.py:534
  62.2 5.2 %collective-permute-start.21 = (f32[8,2048]{1,0:T(8,128)S(1)}, f32[8,2048]{1,0:T(8,128)S(1)}, u32[]{:S(2)}, u32[]{:S(2)}) collective-permute-start(f32[8,2048]{1,0:T(8,128)S(1)} %get-tuple-element.172), channel_id=1, source_target_pairs={{0,16},{8,24},{16,0},{24,8},{1,17},{9,25},{17,1},{25,9},{2,18},{10... | collective-permute-start | bytes 196616 | tf_op jit(solution)/shard_map/weight_and_key_gradients/ppermute | solution.py:534
  63.7 4.3 %collective-permute-start.20 = (f32[8,2048]{1,0:T(8,128)S(1)}, f32[8,2048]{1,0:T(8,128)S(1)}, u32[]{:S(2)}, u32[]{:S(2)}) collective-permute-start(f32[8,2048]{1,0:T(8,128)S(1)} %get-tuple-element.172), channel_id=1, source_target_pairs={{0,8},{8,0},{16,24},{24,16},{1,9},{9,1},{17,25},{25,17},{2,10},{10... | collective-permute-start | bytes 196616 | tf_op jit(solution)/shard_map/weight_and_key_gradients/ppermute | solution.py:534
  68.0 4.3 %collective-permute-start.23 = (f32[8,2048]{1,0:T(8,128)S(1)}, f32[8,2048]{1,0:T(8,128)S(1)}, u32[]{:S(2)}, u32[]{:S(2)}) collective-permute-start(f32[8,2048]{1,0:T(8,128)S(1)} %add_add_fusion), channel_id=1, source_target_pairs={{0,1},{1,0},{2,3},{3,2},{4,5},{5,4},{6,7},{7,6},{8,9},{9,8},{10,11... | collective-permute-start | bytes 196616 | tf_op jit(solution)/shard_map/weight_and_key_gradients/ppermute | solution.py:534
  69.7 5.4 %collective-permute-start.27 = (f32[128,1024]{1,0:T(8,128)S(1)}, f32[128,1024]{1,0:T(8,128)S(1)}, u32[]{:S(2)}, u32[]{:S(2)}) collective-permute-start(f32[128,1024]{1,0:T(8,128)S(1)} %get-tuple-element.197), channel_id=1, source_target_pairs={{0,4},{4,0},{1,5},{5,1},{2,6},{6,2},{3,7},{7,3},{8,12},{12,8},{9,1... | collective-permute-start | bytes 1572872 | tf_op jit(solution)/shard_map/weight_and_key_gradients/ppermute | solution.py:545
  69.7 5.4 %collective-permute-start.28 = (f32[128,1024]{1,0:T(8,128)S(1)}, f32[128,1024]{1,0:T(8,128)S(1)}, u32[]{:S(2)}, u32[]{:S(2)}) collective-permute-start(f32[128,1024]{1,0:T(8,128)S(1)} %get-tuple-element.199), channel_id=1, source_target_pairs={{0,4},{4,0},{1,5},{5,1},{2,6},{6,2},{3,7},{7,3},{8,12},{12,8},{9,1... | collective-permute-start | bytes 1572872 | tf_op jit(solution)/shard_map/weight_and_key_gradients/ppermute | solution.py:545
  72.4 5.2 %collective-permute-start.26 = (f32[8,2048]{1,0:T(8,128)S(1)}, f32[8,2048]{1,0:T(8,128)S(1)}, u32[]{:S(2)}, u32[]{:S(2)}) collective-permute-start(f32[8,2048]{1,0:T(8,128)S(1)} %add.18), channel_id=1, source_target_pairs={{0,2},{1,3},{2,0},{3,1},{4,6},{5,7},{6,4},{7,5},{8,10},{9,11},{10,... | collective-permute-start | bytes 196616 | tf_op jit(solution)/shard_map/weight_and_key_gradients/ppermute | solution.py:534
  77.6 1.3 %collective-permute-start.29 = (f32[8,2048]{1,0:T(8,128)S(1)}, f32[8,2048]{1,0:T(8,128)S(1)}, u32[]{:S(2)}, u32[]{:S(2)}) collective-permute-start(f32[8,2048]{1,0:T(8,128)S(1)} %add.19.refs_0_), channel_id=1, source_target_pairs={{0,4},{4,0},{1,5},{5,1},{2,6},{6,2},{3,7},{7,3},{8,12},{12,8},{9,1... | collective-permute-start | bytes 196616 | tf_op jit(solution)/shard_map/weight_and_key_gradients/ppermute | solution.py:545
